TPU v7x, 256 devices: a whole 4x4x8 slice. The times are simulated.
256 devices in a mesh: src: 16 (over x_lo, y, core), tgt: 16 (over x_hi, z).
Axes of the slice: x: 4 (x_hi: 2, x_lo: 2; x = x_hi * 2 + x_lo), y: 4, z: 8, core: 2. Of those that a mesh axis runs over, the one named last changes fastest.
Arguments:
- src_coords: float32 [3, 98304], P(None, 'src'), may hold values from 0 to 1, as said below
- tgt_coords: float32 [3, 98304], P(None, 'tgt'), may hold values from 0 to 1
- src_scaling: float32 [32, 98304], P('tgt', 'src'), may hold values from 0.25 to 4
- src_mass: float32 [32, 98304], P('tgt', 'src'), may hold values from 0.25 to 4
- tgt_mass: float32 [32, 98304], P(None, 'tgt'), may hold values from 0.25 to 4
Outputs:
- new_src_scaling: float32 [32, 98304], P('tgt', 'src')
- tgt_scaling: float32 [32, 98304], P('src', 'tgt')
Inputs may be any that keep to these rules, and one draw needn't show every extreme that they name: `src_coords`: source points lie in the unit cube.
All inputs are finite; a program needn't handle non-finite values.
Results may differ from a plain program's by a relative error of at most 0.00036.
Values may be sent and summed in bfloat16 or wider, within the bound.
A program may use at most 64 MiB of HBM per device.

v0:
```python
import jax
import jax.numpy as jnp
from jax import lax
from jax.sharding import PartitionSpec as P


def kernel_block(xb, yt):
    dist = (xb[0][:, None] - yt[0][None, :]) ** 2
    dist = dist + (xb[1][:, None] - yt[1][None, :]) ** 2
    dist = dist + (xb[2][:, None] - yt[2][None, :]) ** 2
    return (180.0 * jnp.exp(-100.0 * dist)).astype(jnp.bfloat16)


def on_device(src_coords, tgt_coords, src_scaling, src_mass, tgt_mass):
    src_pts = src_coords.shape[1]
    tgt_pts = tgt_coords.shape[1]
    weights = tgt_mass.shape[0]
    block = min(512, src_pts)
    count = src_pts // block
    xs_blocks = src_coords.reshape(3, count, block).transpose(1, 0, 2)
    src_low = lax.all_gather(src_scaling.astype(jnp.bfloat16), "tgt", axis=0, tiled=True)
    u_blocks = src_low.reshape(weights, count, block).transpose(1, 0, 2)

    def col_step(carry, items):
        xb, ub = items
        kern = kernel_block(xb, tgt_coords)
        return (carry + jnp.dot(ub, kern, preferred_element_type=jnp.float32), None)

    col_terms, _ = lax.scan(
        col_step, jnp.zeros((weights, tgt_pts), jnp.float32), (xs_blocks, u_blocks)
    )
    total_src = src_pts * lax.axis_size("src")
    share_rows = weights // lax.axis_size("src")
    col_part = lax.psum_scatter(col_terms, "src", scatter_dimension=0, tiled=True)
    mass_part = lax.dynamic_slice_in_dim(
        tgt_mass, lax.axis_index("src") * share_rows, share_rows, 0
    )
    tgt_scaling = mass_part / (col_part / total_src)
    tgt_low = lax.all_gather(tgt_scaling.astype(jnp.bfloat16), "src", axis=0, tiled=True)

    def row_step(xb):
        kern = kernel_block(xb, tgt_coords)
        return jnp.dot(tgt_low, kern.T, preferred_element_type=jnp.float32)

    rows = lax.map(row_step, xs_blocks)
    row_terms = rows.transpose(1, 0, 2).reshape(weights, src_pts)
    row_part = lax.psum_scatter(row_terms, "tgt", scatter_dimension=0, tiled=True)
    total_tgt = tgt_pts * lax.axis_size("tgt")
    new_src_scaling = src_mass / (row_part / total_tgt)
    return (new_src_scaling, tgt_scaling)


def solution(mesh):
    placed = (P(None, "src"), P(None, "tgt"), P("tgt", "src"), P("tgt", "src"), P(None, "tgt"))
    return jax.shard_map(
        on_device,
        mesh=mesh,
        in_specs=placed,
        out_specs=(P("tgt", "src"), P("src", "tgt")),
        check_vma=False,
    )
```

profile of v0, /device:TPU:16, one launch (start us, length us, event | category | flops | bytes accessed | tf_op | source)
XLA Modules:
  0.0 511.5 jit_solution(1430984514631784748)
XLA Ops:
  8.0 46.1 %all-gather = bf16[16,2,6144]{2,1,0:T(2,128)(2,1)S(1)} all-gather(bf16[1,2,6144]{2,1,0:T(2,128)(2,1)S(1)} %convert_bitcast_fusion.1), channel_id=1, replica_groups=mesh['src'=16,'tgt'=16] {'tgt'}, dimensions={0}, use_global_device_ids=true | all-gather | bytes 417792 | tf_op jit(solution)/shard_map/all_gather | solution.py:21
  55.1 77.2 %while.22 = (s32[]{:T(128)}, f32[32,6144]{1,0:T(8,128)S(1)}, bf16[12,32,512]{2,1,0:T(8,128)(2,1)S(1)}, f32[12,3,512]{2,1,0:T(4,128)}, f32[3,6144]{1,0:T(4,128)S(1)}, /*index=5*/s32[]{:T(128)}, s32[]{:T(128)}, s32[]{}, s32[]{}) while((s32[]{:T(128)}, f32[32,6144]{1,0:T(8,128)S(1)}, bf16[12,32,512]{2,1,0:T(8,128)(2,1)S(1)}, ...), condition=%wide.region_1.2_spmd.clone, body=%wide.region_0.1_spmd.clone.sunk | while | flops 236322816 | bytes 1845391 | solution.py:29
  55.9 5.5 %convolution_add_fusion.2 = f32[32,6144]{1,0:T(8,128)S(1)} fusion(f32[6144]{0:T(1024)S(1)} %bitcast.69, f32[512]{0:T(512)S(1)} %bitcast.76, f32[6144]{0:T(1024)S(1)} %bitcast.70, f32[512]{0:T(512)S(1)} %bitcast.75, f32[6144]{0:T(1024)S(1)} %bitcast.68, f32[512]{0:T(512)S(1)} %bitcast.74, f32[32,6144]{1,0:T(8,128)S(1)} %get-tuple-element.216, ...), kind=kOutput, calls=%fused_computation.10.clone.1 | convolution fusion | flops 236322816 | bytes 1685509 | tf_op jit(solution)/shard_map/while/body/eval_jaxpr/dot_general | solution.py:27
  62.4 5.5 %convolution_add_fusion.2 = f32[32,6144]{1,0:T(8,128)S(1)} fusion(f32[6144]{0:T(1024)S(1)} %bitcast.69, f32[512]{0:T(512)S(1)} %bitcast.76, f32[6144]{0:T(1024)S(1)} %bitcast.70, f32[512]{0:T(512)S(1)} %bitcast.75, f32[6144]{0:T(1024)S(1)} %bitcast.68, f32[512]{0:T(512)S(1)} %bitcast.74, f32[32,6144]{1,0:T(8,128)S(1)} %get-tuple-element.216, ...), kind=kOutput, calls=%fused_computation.10.clone.1 | convolution fusion | flops 236322816 | bytes 1685509 | tf_op jit(solution)/shard_map/while/body/eval_jaxpr/dot_general | solution.py:27
  68.8 5.5 %convolution_add_fusion.2 = f32[32,6144]{1,0:T(8,128)S(1)} fusion(f32[6144]{0:T(1024)S(1)} %bitcast.69, f32[512]{0:T(512)S(1)} %bitcast.76, f32[6144]{0:T(1024)S(1)} %bitcast.70, f32[512]{0:T(512)S(1)} %bitcast.75, f32[6144]{0:T(1024)S(1)} %bitcast.68, f32[512]{0:T(512)S(1)} %bitcast.74, f32[32,6144]{1,0:T(8,128)S(1)} %get-tuple-element.216, ...), kind=kOutput, calls=%fused_computation.10.clone.1 | convolution fusion | flops 236322816 | bytes 1685509 | tf_op jit(solution)/shard_map/while/body/eval_jaxpr/dot_general | solution.py:27
  75.2 5.5 %convolution_add_fusion.2 = f32[32,6144]{1,0:T(8,128)S(1)} fusion(f32[6144]{0:T(1024)S(1)} %bitcast.69, f32[512]{0:T(512)S(1)} %bitcast.76, f32[6144]{0:T(1024)S(1)} %bitcast.70, f32[512]{0:T(512)S(1)} %bitcast.75, f32[6144]{0:T(1024)S(1)} %bitcast.68, f32[512]{0:T(512)S(1)} %bitcast.74, f32[32,6144]{1,0:T(8,128)S(1)} %get-tuple-element.216, ...), kind=kOutput, calls=%fused_computation.10.clone.1 | convolution fusion | flops 236322816 | bytes 1685509 | tf_op jit(solution)/shard_map/while/body/eval_jaxpr/dot_general | solution.py:27
  81.7 5.5 %convolution_add_fusion.2 = f32[32,6144]{1,0:T(8,128)S(1)} fusion(f32[6144]{0:T(1024)S(1)} %bitcast.69, f32[512]{0:T(512)S(1)} %bitcast.76, f32[6144]{0:T(1024)S(1)} %bitcast.70, f32[512]{0:T(512)S(1)} %bitcast.75, f32[6144]{0:T(1024)S(1)} %bitcast.68, f32[512]{0:T(512)S(1)} %bitcast.74, f32[32,6144]{1,0:T(8,128)S(1)} %get-tuple-element.216, ...), kind=kOutput, calls=%fused_computation.10.clone.1 | convolution fusion | flops 236322816 | bytes 1685509 | tf_op jit(solution)/shard_map/while/body/eval_jaxpr/dot_general | solution.py:27
  88.1 5.5 %convolution_add_fusion.2 = f32[32,6144]{1,0:T(8,128)S(1)} fusion(f32[6144]{0:T(1024)S(1)} %bitcast.69, f32[512]{0:T(512)S(1)} %bitcast.76, f32[6144]{0:T(1024)S(1)} %bitcast.70, f32[512]{0:T(512)S(1)} %bitcast.75, f32[6144]{0:T(1024)S(1)} %bitcast.68, f32[512]{0:T(512)S(1)} %bitcast.74, f32[32,6144]{1,0:T(8,128)S(1)} %get-tuple-element.216, ...), kind=kOutput, calls=%fused_computation.10.clone.1 | convolution fusion | flops 236322816 | bytes 1685509 | tf_op jit(solution)/shard_map/while/body/eval_jaxpr/dot_general | solution.py:27
  94.5 5.5 %convolution_add_fusion.2 = f32[32,6144]{1,0:T(8,128)S(1)} fusion(f32[6144]{0:T(1024)S(1)} %bitcast.69, f32[512]{0:T(512)S(1)} %bitcast.76, f32[6144]{0:T(1024)S(1)} %bitcast.70, f32[512]{0:T(512)S(1)} %bitcast.75, f32[6144]{0:T(1024)S(1)} %bitcast.68, f32[512]{0:T(512)S(1)} %bitcast.74, f32[32,6144]{1,0:T(8,128)S(1)} %get-tuple-element.216, ...), kind=kOutput, calls=%fused_computation.10.clone.1 | convolution fusion | flops 236322816 | bytes 1685509 | tf_op jit(solution)/shard_map/while/body/eval_jaxpr/dot_general | solution.py:27
  101.0 5.5 %convolution_add_fusion.2 = f32[32,6144]{1,0:T(8,128)S(1)} fusion(f32[6144]{0:T(1024)S(1)} %bitcast.69, f32[512]{0:T(512)S(1)} %bitcast.76, f32[6144]{0:T(1024)S(1)} %bitcast.70, f32[512]{0:T(512)S(1)} %bitcast.75, f32[6144]{0:T(1024)S(1)} %bitcast.68, f32[512]{0:T(512)S(1)} %bitcast.74, f32[32,6144]{1,0:T(8,128)S(1)} %get-tuple-element.216, ...), kind=kOutput, calls=%fused_computation.10.clone.1 | convolution fusion | flops 236322816 | bytes 1685509 | tf_op jit(solution)/shard_map/while/body/eval_jaxpr/dot_general | solution.py:27
  107.4 5.5 %convolution_add_fusion.2 = f32[32,6144]{1,0:T(8,128)S(1)} fusion(f32[6144]{0:T(1024)S(1)} %bitcast.69, f32[512]{0:T(512)S(1)} %bitcast.76, f32[6144]{0:T(1024)S(1)} %bitcast.70, f32[512]{0:T(512)S(1)} %bitcast.75, f32[6144]{0:T(1024)S(1)} %bitcast.68, f32[512]{0:T(512)S(1)} %bitcast.74, f32[32,6144]{1,0:T(8,128)S(1)} %get-tuple-element.216, ...), kind=kOutput, calls=%fused_computation.10.clone.1 | convolution fusion | flops 236322816 | bytes 1685509 | tf_op jit(solution)/shard_map/while/body/eval_jaxpr/dot_general | solution.py:27
  113.8 5.5 %convolution_add_fusion.2 = f32[32,6144]{1,0:T(8,128)S(1)} fusion(f32[6144]{0:T(1024)S(1)} %bitcast.69, f32[512]{0:T(512)S(1)} %bitcast.76, f32[6144]{0:T(1024)S(1)} %bitcast.70, f32[512]{0:T(512)S(1)} %bitcast.75, f32[6144]{0:T(1024)S(1)} %bitcast.68, f32[512]{0:T(512)S(1)} %bitcast.74, f32[32,6144]{1,0:T(8,128)S(1)} %get-tuple-element.216, ...), kind=kOutput, calls=%fused_computation.10.clone.1 | convolution fusion | flops 236322816 | bytes 1685509 | tf_op jit(solution)/shard_map/while/body/eval_jaxpr/dot_general | solution.py:27
  120.3 5.5 %convolution_add_fusion.2 = f32[32,6144]{1,0:T(8,128)S(1)} fusion(f32[6144]{0:T(1024)S(1)} %bitcast.69, f32[512]{0:T(512)S(1)} %bitcast.76, f32[6144]{0:T(1024)S(1)} %bitcast.70, f32[512]{0:T(512)S(1)} %bitcast.75, f32[6144]{0:T(1024)S(1)} %bitcast.68, f32[512]{0:T(512)S(1)} %bitcast.74, f32[32,6144]{1,0:T(8,128)S(1)} %get-tuple-element.216, ...), kind=kOutput, calls=%fused_computation.10.clone.1 | convolution fusion | flops 236322816 | bytes 1685509 | tf_op jit(solution)/shard_map/while/body/eval_jaxpr/dot_general | solution.py:27
  126.7 5.5 %convolution_add_fusion.2 = f32[32,6144]{1,0:T(8,128)S(1)} fusion(f32[6144]{0:T(1024)S(1)} %bitcast.69, f32[512]{0:T(512)S(1)} %bitcast.76, f32[6144]{0:T(1024)S(1)} %bitcast.70, f32[512]{0:T(512)S(1)} %bitcast.75, f32[6144]{0:T(1024)S(1)} %bitcast.68, f32[512]{0:T(512)S(1)} %bitcast.74, f32[32,6144]{1,0:T(8,128)S(1)} %get-tuple-element.216, ...), kind=kOutput, calls=%fused_computation.10.clone.1 | convolution fusion | flops 236322816 | bytes 1685509 | tf_op jit(solution)/shard_map/while/body/eval_jaxpr/dot_general | solution.py:27
  134.5 111.5 %all-reduce.5.cloned.1.call-done = f32[32,6144]{1,0:T(8,128)} async-done(((f32[32,6144]{1,0:T(8,128)}), f32[32,6144]{1,0:T(8,128)}) %all-reduce.5.cloned.1.call-update) | async-done | bytes 786448
  247.7 19.6 %all-gather.1 = bf16[16,2,6144]{2,1,0:T(2,128)(2,1)S(1)} all-gather(bf16[1,2,6144]{2,1,0:T(2,128)(2,1)S(1)} %get-tuple-element.106), channel_id=1, replica_groups=mesh['src'=16,'tgt'=16] {'src'}, dimensions={0}, use_global_device_ids=true | all-gather | bytes 417792 | tf_op jit(solution)/shard_map/all_gather | solution.py:39
  267.5 74.0 %while.21 = (s32[]{:T(128)}, f32[12,32,512]{2,1,0:T(8,128)S(1)}, f32[12,3,512]{2,1,0:T(4,128)}, f32[3,6144]{1,0:T(4,128)S(1)}, bf16[32,6144]{1,0:T(8,128)(2,1)S(1)}, /*index=5*/s32[]{:T(128)}, s32[]{:T(128)}, s32[]{}, s32[]{}) while((s32[]{:T(128)}, f32[12,32,512]{2,1,0:T(8,128)S(1)}, f32[12,3,512]{2,1,0:T(4,128)}, f32[3,6144]{1,0:T(4,128)S(1)}, ...), condition=%wide.region_4.5_spmd, body=%wide.region_3.4_spmd.sunk | while | flops 235929600 | bytes 698501 | solution.py:45
  268.4 5.3 %fusion.30 = f32[12,32,512]{2,1,0:T(8,128)S(1)} fusion(f32[12,32,512]{2,1,0:T(8,128)S(1)} %get-tuple-element.243, s32[]{:T(128)} %get-tuple-element.242, bf16[32,6144]{1,0:T(8,128)(2,1)S(1)} %get-tuple-element.255, f32[6144]{0:T(1024)S(1)} %bitcast.72, f32[512]{0:T(512)S(1)} %bitcast.79, f32[6144]{0:T(1024)S(1)} %bitcast.73, f32[512]{0:T(512)S(1)} %bitcast.78, ...), kind=kOutput, calls=%fused_computation.3.clone.1 | convolution fusion | flops 235929600 | bytes 538628 | tf_op jit(solution)/shard_map/while/body/eval_jaxpr/dot_general | solution.py:43
  274.5 5.3 %fusion.30 = f32[12,32,512]{2,1,0:T(8,128)S(1)} fusion(f32[12,32,512]{2,1,0:T(8,128)S(1)} %get-tuple-element.243, s32[]{:T(128)} %get-tuple-element.242, bf16[32,6144]{1,0:T(8,128)(2,1)S(1)} %get-tuple-element.255, f32[6144]{0:T(1024)S(1)} %bitcast.72, f32[512]{0:T(512)S(1)} %bitcast.79, f32[6144]{0:T(1024)S(1)} %bitcast.73, f32[512]{0:T(512)S(1)} %bitcast.78, ...), kind=kOutput, calls=%fused_computation.3.clone.1 | convolution fusion | flops 235929600 | bytes 538628 | tf_op jit(solution)/shard_map/while/body/eval_jaxpr/dot_general | solution.py:43
  280.7 5.3 %fusion.30 = f32[12,32,512]{2,1,0:T(8,128)S(1)} fusion(f32[12,32,512]{2,1,0:T(8,128)S(1)} %get-tuple-element.243, s32[]{:T(128)} %get-tuple-element.242, bf16[32,6144]{1,0:T(8,128)(2,1)S(1)} %get-tuple-element.255, f32[6144]{0:T(1024)S(1)} %bitcast.72, f32[512]{0:T(512)S(1)} %bitcast.79, f32[6144]{0:T(1024)S(1)} %bitcast.73, f32[512]{0:T(512)S(1)} %bitcast.78, ...), kind=kOutput, calls=%fused_computation.3.clone.1 | convolution fusion | flops 235929600 | bytes 538628 | tf_op jit(solution)/shard_map/while/body/eval_jaxpr/dot_general | solution.py:43
  286.9 5.3 %fusion.30 = f32[12,32,512]{2,1,0:T(8,128)S(1)} fusion(f32[12,32,512]{2,1,0:T(8,128)S(1)} %get-tuple-element.243, s32[]{:T(128)} %get-tuple-element.242, bf16[32,6144]{1,0:T(8,128)(2,1)S(1)} %get-tuple-element.255, f32[6144]{0:T(1024)S(1)} %bitcast.72, f32[512]{0:T(512)S(1)} %bitcast.79, f32[6144]{0:T(1024)S(1)} %bitcast.73, f32[512]{0:T(512)S(1)} %bitcast.78, ...), kind=kOutput, calls=%fused_computation.3.clone.1 | convolution fusion | flops 235929600 | bytes 538628 | tf_op jit(solution)/shard_map/while/body/eval_jaxpr/dot_general | solution.py:43
  293.0 5.3 %fusion.30 = f32[12,32,512]{2,1,0:T(8,128)S(1)} fusion(f32[12,32,512]{2,1,0:T(8,128)S(1)} %get-tuple-element.243, s32[]{:T(128)} %get-tuple-element.242, bf16[32,6144]{1,0:T(8,128)(2,1)S(1)} %get-tuple-element.255, f32[6144]{0:T(1024)S(1)} %bitcast.72, f32[512]{0:T(512)S(1)} %bitcast.79, f32[6144]{0:T(1024)S(1)} %bitcast.73, f32[512]{0:T(512)S(1)} %bitcast.78, ...), kind=kOutput, calls=%fused_computation.3.clone.1 | convolution fusion | flops 235929600 | bytes 538628 | tf_op jit(solution)/shard_map/while/body/eval_jaxpr/dot_general | solution.py:43
  299.2 5.3 %fusion.30 = f32[12,32,512]{2,1,0:T(8,128)S(1)} fusion(f32[12,32,512]{2,1,0:T(8,128)S(1)} %get-tuple-element.243, s32[]{:T(128)} %get-tuple-element.242, bf16[32,6144]{1,0:T(8,128)(2,1)S(1)} %get-tuple-element.255, f32[6144]{0:T(1024)S(1)} %bitcast.72, f32[512]{0:T(512)S(1)} %bitcast.79, f32[6144]{0:T(1024)S(1)} %bitcast.73, f32[512]{0:T(512)S(1)} %bitcast.78, ...), kind=kOutput, calls=%fused_computation.3.clone.1 | convolution fusion | flops 235929600 | bytes 538628 | tf_op jit(solution)/shard_map/while/body/eval_jaxpr/dot_general | solution.py:43
  344.4 158.6 %all-reduce.7.cloned.1.call-done = f32[32,6144]{1,0:T(8,128)} async-done(((f32[32,6144]{1,0:T(8,128)}), f32[32,6144]{1,0:T(8,128)}) %all-reduce.7.cloned.1.call-update) | async-done | bytes 786448
  (79 shorter events, 61.6 us)
Async XLA Ops:
  7.2 238.8 %all-reduce.5.cloned.1.call-start = ((), (), s32[]{:S(2)}) async-start(), calls=%async_computation | async-start | bytes 1572864
  54.2 0.9 copy-start
  132.3 0.9 copy-start.1
  132.3 1.0 copy-start.4
  133.2 369.8 %all-reduce.7.cloned.1.call-start = ((), (), s32[]{:S(2)}) async-start(), calls=%async_computation.1 | async-start | bytes 1572864
  342.5 0.7 copy-start.3
  342.5 160.6 %copy-start.2 = (f32[2,6144]{1,0:T(2,128)S(1)}, f32[2,6144]{1,0:T(2,128)}, u32[]{:S(2)}) copy-start(f32[2,6144]{1,0:T(2,128)} %param.12) | copy-start | bytes 147460
Sparse Core Ops, SparseCore 0:
  133.3 112.6 all-reduce.4
  342.6 160.3 all-reduce.6
where the time goes:
time: 513 us; the launch traced here: 511 us
  waiting for transfers between devices  270 us (53%)
  matrix products  130 us (25%)
  blocking collectives  65.7 us (13%)
  local copies, waits for them, and re-layouts  25.7 us (5%)
  between operations  15.4 us (3%)
    unnamed x4, waiting for transfers between devices  270 us
    dot_general x12, matrix products, col_step(): return (carry + jnp.dot(ub, kern, preferred_element_type=jnp.float32), None)  66.3 us
    dot_general x12, matrix products, row_step(): return jnp.dot(tgt_low, kern.T, preferred_element_type=jnp.float32)  63.4 us
    all_gather x1, blocking collectives, on_device(): lax.all_gather(src_scaling.astype(jnp.bfloat16), 'tgt', axis=0, tiled=True)  46.1 us
    slice x48, local copies, waits for them, and re-layouts, kernel_block(): dist = (xb[0][:, None] - yt[0][None, :]) ** 2  21 us
    all_gather x1, blocking collectives, on_device(): lax.all_gather(tgt_scaling.astype(jnp.bfloat16), 'src', axis=0, tiled=True)  19.6 us
  transfers between devices with their start and end apart: 2, of which 2 were waited for; matrix products, arithmetic and copies ran while one was open for 0% of the time, Pallas kernels for 0%

commit v1 on v0

v1 whole, which is shorter than its diff:
```python
import functools
import math

import jax
import jax.numpy as jnp
from jax import lax
from jax.experimental import pallas as pl
from jax.experimental.pallas import tpu as pltpu
from jax.sharding import PartitionSpec as P

F32, BF16 = jnp.float32, jnp.bfloat16
MESH = pl.DeviceIdType.MESH
RATE = 100.0 / math.log(2.0)
TILE = 1024
CHUNKS = 3
DEPTH = 32


def split3(values):
    first = lax.reduce_precision(values, 8, 7)
    rest = values - first
    second = lax.reduce_precision(rest, 8, 7)
    return first, second, lax.reduce_precision(rest - second, 8, 7)


def factors(src_coords, tgt_coords):
    xc, yc = src_coords - 0.5, tgt_coords - 0.5
    xs, ys = split3(2.0 * RATE * xc), split3(yc)
    xa = split3(-RATE * jnp.sum(xc * xc, 0, keepdims=True))
    yb = split3(math.log2(180.0) - RATE * jnp.sum(yc * yc, 0, keepdims=True))
    left, right = [], []
    for p, q in ((0, 0), (0, 1), (1, 0), (1, 1), (0, 2), (2, 0), (1, 2), (2, 1)):
        left.append(xs[p])
        right.append(ys[q])
    for part in range(3):
        left += [xa[part], jnp.ones_like(xa[part])]
        right += [jnp.ones_like(yb[part]), yb[part]]
    left, right = jnp.concatenate(left, 0), jnp.concatenate(right, 0)
    pad = ((0, DEPTH - left.shape[0]), (0, 0))
    return jnp.pad(left, pad).astype(BF16).T, jnp.pad(right, pad).astype(BF16)


def fold(rows):
    n = rows.shape[1]
    return rows.reshape(2, CHUNKS, 8, n // (8 * CHUNKS)).transpose(1, 0, 2, 3).reshape(CHUNKS, 16, n // (8 * CHUNKS))


def unfold(parts):
    wide = parts.shape[2]
    return parts.reshape(CHUNKS, 2, 8, wide).transpose(1, 0, 2, 3).reshape(2, CHUNKS * 8 * wide)


def kernel(
    total, x_ref, y_ref, u_ref, cm_ref, rm_ref,
    new_ref, tgt_ref, far_ref,
    near, stage, u_in, v_in, u_all, v_all, shuffle, col_acc, row_acc, col_out, row_out, col_in, row_in,
    stage_sem, u_send, u_recv, v_send, v_recv, col_send, col_recv, row_send, row_recv,
):
    src, tgt = lax.axis_index("src"), lax.axis_index("tgt")
    peers = lax.axis_size("src")
    blocks = y_ref.shape[1] // TILE
    tiles = x_ref.shape[0] // TILE
    wide = u_ref.shape[2]
    span = 8 * wide
    stored = near.shape[0]
    far = blocks - stored

    def each_peer(body):
        def step(r, carry):
            body(r)
            return carry
        lax.fori_loop(1, peers, step, 0)

    barrier = pltpu.get_barrier_semaphore()

    def greet(r):
        pl.semaphore_signal(barrier, inc=1, device_id={"src": lax.rem(src + r, peers)}, device_id_type=MESH)
        pl.semaphore_signal(barrier, inc=1, device_id={"tgt": lax.rem(tgt + r, peers)}, device_id_type=MESH)

    each_peer(greet)
    u_in[tgt] = u_ref[...]
    pl.semaphore_wait(barrier, 2 * (peers - 1))

    def gather_copy(buf, axis, me, r, send, recv):
        return pltpu.make_async_remote_copy(
            src_ref=buf.at[me], dst_ref=buf.at[me], send_sem=send, recv_sem=recv,
            device_id={axis: lax.rem(me + r, peers)}, device_id_type=MESH,
        )

    def scatter_copy(out, into, axis, me, r, send, recv):
        peer = lax.rem(me + r, peers)
        return pltpu.make_async_remote_copy(
            src_ref=out.at[peer], dst_ref=into.at[r - 1], send_sem=send, recv_sem=recv,
            device_id={axis: peer}, device_id_type=MESH,
        )

    def wait_all(buf, axis, me, send, recv):
        group = buf.at[pl.ds(0, peers - 1)]
        copy = pltpu.make_async_remote_copy(
            src_ref=group, dst_ref=group, send_sem=send, recv_sem=recv,
            device_id={axis: lax.rem(me + 1, peers)}, device_id_type=MESH,
        )
        return copy

    each_peer(lambda r: gather_copy(u_in, "tgt", tgt, r, u_send, u_recv).start())

    def rows_at(i):
        return pl.ds(pl.multiple_of(i * TILE, TILE), TILE)

    def make_tile(b, i):
        e = jnp.dot(x_ref[rows_at(i), :], y_ref[:, b * TILE:(b + 1) * TILE], preferred_element_type=F32)
        return jnp.exp2(e).astype(BF16)

    def ordered(parts, all_ref, at):
        for d in range(peers):
            part = parts(d).astype(F32)
            for h in range(wide // 128):
                shuffle[h, d * 16:(d + 1) * 16, :] = part[:, h * 128:(h + 1) * 128]
        for k in range(8):
            for h in range(wide // 128):
                lanes = at + k * wide + h * 128
                all_ref[:, lanes:lanes + 128] = shuffle[h, pl.ds(k, 2 * peers, stride=8), :].astype(BF16)

    def scattered(acc, at, out):
        for k in range(8):
            for h in range(wide // 128):
                lanes = at + k * wide + h * 128
                shuffle[h, pl.ds(k, 2 * peers, stride=8), :] = acc[:, lanes:lanes + 128]
        for d in range(peers):
            for h in range(wide // 128):
                out[d, :, h * 128:(h + 1) * 128] = shuffle[h, d * 16:(d + 1) * 16, :]

    def summed(out, into, me):
        value = out[me]
        for r in range(peers - 1):
            value = value + into[r]
        return value

    def make_only(b):
        def step(i, carry):
            near[b - far, rows_at(i), :] = make_tile(b, i)
            return carry
        lax.fori_loop(0, tiles, step, 0)

    def use_only(b):
        def step(i, acc):
            return acc + jnp.dot(u_all[:, rows_at(i)], near[b - far, rows_at(i), :], preferred_element_type=F32)
        col_acc[:, b * TILE:(b + 1) * TILE] = lax.fori_loop(0, tiles, step, jnp.zeros((2 * peers, TILE), F32))

    def make_and_use(b):
        def step(i, acc):
            tile = make_tile(b, i)
            if b >= far:
                near[b - far, rows_at(i), :] = tile
            else:
                slot = lax.rem(i, 3)
                if b == 0:
                    @pl.when(i >= 3)
                    def _():
                        pltpu.make_async_copy(stage.at[slot], far_ref.at[b, 0], stage_sem.at[slot]).wait()
                else:
                    pltpu.make_async_copy(stage.at[slot], far_ref.at[b, 0], stage_sem.at[slot]).wait()
                stage[slot] = tile
                pltpu.make_async_copy(stage.at[slot], far_ref.at[b, i], stage_sem.at[slot]).start()
            return acc + jnp.dot(u_all[:, rows_at(i)], tile, preferred_element_type=F32)
        col_acc[:, b * TILE:(b + 1) * TILE] = lax.fori_loop(0, tiles, step, jnp.zeros((2 * peers, TILE), F32))

    def send_cols(c):
        scattered(col_acc, c * span, col_out.at[c])
        each_peer(lambda r: scatter_copy(col_out.at[c], col_in.at[c], "src", src, r, col_send.at[c], col_recv.at[c]).start())

    def turn_cols(c):
        wait_all(col_in.at[c], "src", src, col_send.at[c], col_recv.at[c]).wait_recv()
        value = cm_ref[c] / (summed(col_out.at[c], col_in.at[c], src) / total)
        tgt_ref[c] = value
        v_in[c, src] = value.astype(BF16)
        each_peer(lambda r: gather_copy(v_in.at[c], "src", src, r, v_send.at[c], v_recv.at[c]).start())

    def take_cols(c):
        wait_all(v_in.at[c], "src", src, v_send.at[c], v_recv.at[c]).wait_recv()
        ordered(lambda d: v_in[c, d], v_all, c * span)

    make_only(3)
    make_only(4)
    wait_all(u_in, "tgt", tgt, u_send, u_recv).wait_recv()
    for c in range(CHUNKS):
        ordered(lambda d: u_in[d, c], u_all, c * span)
    make_and_use(0)
    make_and_use(1)
    send_cols(0)
    make_and_use(2)
    use_only(3)
    send_cols(1)
    turn_cols(0)
    use_only(4)
    make_and_use(5)
    send_cols(2)
    turn_cols(1)

    count = far * tiles

    def fetch(t):
        slot = lax.rem(t, 3)
        return pltpu.make_async_copy(far_ref.at[lax.div(t, tiles), lax.rem(t, tiles)], stage.at[slot], stage_sem.at[slot])

    for slot in range(3):
        pltpu.make_async_copy(stage.at[slot], far_ref.at[far - 1, 0], stage_sem.at[slot]).wait()
    for t in range(3):
        fetch(t).start()

    def far_block(b):
        def step(i, carry):
            t = b * tiles + i
            fetch(t).wait()
            part = lax.dot_general(
                v_all[:, b * TILE:(b + 1) * TILE], stage[lax.rem(t, 3)], (((1,), (1,)), ((), ())), preferred_element_type=F32
            )
            if b == 0:
                row_acc[:, rows_at(i)] = part
            else:
                row_acc[:, rows_at(i)] += part

            @pl.when(t + 3 < count)
            def _():
                fetch(t + 3).start()
            return carry
        lax.fori_loop(0, tiles, step, 0)

    take_cols(0)
    far_block(0)
    turn_cols(2)
    far_block(1)
    take_cols(1)
    far_block(2)
    take_cols(2)
    per = span // TILE
    for c in range(CHUNKS):
        def step(i, carry):
            part = row_acc[:, rows_at(i)]
            for b in range(far, blocks):
                part = part + lax.dot_general(
                    v_all[:, b * TILE:(b + 1) * TILE], near[b - far, rows_at(i), :], (((1,), (1,)), ((), ())),
                    preferred_element_type=F32,
                )
            row_acc[:, rows_at(i)] = part
            return carry
        lax.fori_loop(c * per, (c + 1) * per, step, 0)
        scattered(row_acc, c * span, row_out.at[c])
        each_peer(lambda r: scatter_copy(row_out.at[c], row_in.at[c], "tgt", tgt, r, row_send.at[c], row_recv.at[c]).start())
    for c in range(CHUNKS):
        wait_all(row_in.at[c], "tgt", tgt, row_send.at[c], row_recv.at[c]).wait_recv()
        new_ref[c] = rm_ref[c] / (summed(row_out.at[c], row_in.at[c], tgt) / total)
    wait_all(u_in, "tgt", tgt, u_send, u_recv).wait_send()
    for c in range(CHUNKS):
        wait_all(col_in.at[c], "src", src, col_send.at[c], col_recv.at[c]).wait_send()
        wait_all(v_in.at[c], "src", src, v_send.at[c], v_recv.at[c]).wait_send()
        wait_all(row_in.at[c], "tgt", tgt, row_send.at[c], row_recv.at[c]).wait_send()


def on_device(src_coords, tgt_coords, src_scaling, src_mass, tgt_mass):
    pts = src_coords.shape[1]
    peers = lax.axis_size("src")
    total = float(pts * peers)
    x, y = factors(src_coords, tgt_coords)
    mass = lax.dynamic_slice_in_dim(tgt_mass, lax.axis_index("src") * 2, 2, 0)
    wide = pts // (8 * CHUNKS)
    blocks, tiles = pts // TILE, pts // TILE
    stored = blocks // 2
    vmem = pl.BlockSpec(memory_space=pltpu.VMEM)
    dma = pltpu.SemaphoreType.DMA
    new, out, _ = pl.pallas_call(
        functools.partial(kernel, total),
        out_shape=(
            jax.ShapeDtypeStruct((CHUNKS, 16, wide), F32),
            jax.ShapeDtypeStruct((CHUNKS, 16, wide), F32),
            jax.ShapeDtypeStruct((blocks - stored, tiles, TILE, TILE), BF16),
        ),
        in_specs=[vmem] * 5,
        out_specs=(vmem, vmem, pl.BlockSpec(memory_space=pl.ANY)),
        scratch_shapes=[
            pltpu.VMEM((stored, pts, TILE), BF16),
            pltpu.VMEM((3, TILE, TILE), BF16),
            pltpu.VMEM((peers, CHUNKS, 16, wide), BF16),
            pltpu.VMEM((CHUNKS, peers, 16, wide), BF16),
            pltpu.VMEM((2 * peers, pts), BF16),
            pltpu.VMEM((2 * peers, pts), BF16),
            pltpu.VMEM((wide // 128, 16 * peers, 128), F32),
            pltpu.VMEM((2 * peers, pts), F32),
            pltpu.VMEM((2 * peers, pts), F32),
            pltpu.VMEM((CHUNKS, peers, 16, wide), F32),
            pltpu.VMEM((CHUNKS, peers, 16, wide), F32),
            pltpu.VMEM((CHUNKS, peers - 1, 16, wide), F32),
            pltpu.VMEM((CHUNKS, peers - 1, 16, wide), F32),
            dma((3,)), dma, dma, dma((CHUNKS,)), dma((CHUNKS,)),
            dma((CHUNKS,)), dma((CHUNKS,)), dma((CHUNKS,)), dma((CHUNKS,)),
        ],
        compiler_params=pltpu.CompilerParams(
            collective_id=0, has_side_effects=True, vmem_limit_bytes=60 * 2**20
        ),
    )(x, y, fold(src_scaling.astype(BF16)), fold(mass), fold(src_mass))
    return unfold(new), unfold(out)


def solution(mesh):
    placed = (P(None, "src"), P(None, "tgt"), P("tgt", "src"), P("tgt", "src"), P(None, "tgt"))
    return jax.shard_map(
        on_device,
        mesh=mesh,
        in_specs=placed,
        out_specs=(P("tgt", "src"), P("src", "tgt")),
        check_vma=False,
    )
```

time: 513 us -> 113 us (0.22)
  waiting for transfers between devices: 270 us -> 0 us
  matrix products: 130 us -> 0 us
  Pallas kernels: 0 us -> 97.7 us
  blocking collectives: 65.7 us -> 0 us
  local copies, waits for them, and re-layouts: 25.7 us -> 10 us
  between operations: 15.4 us -> 0.73 us
    unnamed x4 -> x0, waiting for transfers between devices: 270 us -> none
    dot_general x24 -> x0, matrix products: 130 us -> none  [the longest x12 66.3 us: col_step(): return (carry + jnp.dot(ub, kern, preferred_element_type=jnp.float32), None)]
    pallas_call x0 -> x1, Pallas kernels: none -> 97.7 us  [on_device(): pl.pallas_call(functools.partial(kernel, total), out_shape=(jax.ShapeDtyp...]
    all_gather x2 -> x0, blocking collectives: 65.7 us -> none  [the longest x1 46.1 us: on_device(): lax.all_gather(src_scaling.astype(jnp.bfloat16), 'tgt', axis=0, tiled=True)]
    slice x48 -> x0, local copies, waits for them, and re-layouts: 21 us -> none  [kernel_block(): dist = (xb[0][:, None] - yt[0][None, :]) ** 2]
  transfers between devices with their start and end apart: 2 -> 0, of which waited for: 2 -> 0; matrix products, arithmetic and copies ran while one was open for 0% -> 0% of each run, Pallas kernels for 0% -> 0%
where the time goes in v1:
time: 113 us; the launch traced here: 112 us
  Pallas kernels  97.7 us (86%)
  local copies, waits for them, and re-layouts  10 us (9%)
  other arithmetic  3.04 us (3%)
    pallas_call x1, Pallas kernels, on_device(): pl.pallas_call(functools.partial(kernel, total), out_shape=(jax.ShapeDtyp...  97.7 us
    unnamed x6, local copies, waits for them, and re-layouts  2.9 us
    reshape x3, local copies, waits for them, and re-layouts, fold(): rows.reshape(2, CHUNKS, 8, n // (8 * CHUNKS)).transpose(1, 0, 2, 3)  2.65 us

profile of v1, /device:TPU:16, one launch (start us, length us, event | category | flops | bytes accessed | tf_op | source)
XLA Modules:
  0.0 111.5 jit_solution(12184554734657746345)
XLA Ops:
  0.6 0.0 copy-start
  0.7 0.9 convert_element_type.8
  1.5 0.6 copy_bitcast_fusion.6.u_ref
  2.1 0.0 copy-done
  2.2 0.6 copy_bitcast_fusion.4.cm_ref
  2.8 1.4 %copy_bitcast_fusion.3.rm_ref = f32[3,16,256]{2,1,0:T(8,128)} fusion(f32[1,2,24,256]{3,1,2,0:T(2,128)} %bitcast.54), kind=kLoop, calls=%fused_computation.19 | loop fusion | bytes 98304 | tf_op jit(solution)/shard_map/reshape | solution.py:45
  4.2 1.0 multiply_reduce_fusion.1
  5.3 0.1 fusion.5
  5.3 1.1 concatenate.8
  6.4 1.0 multiply_reduce_fusion
  7.5 0.1 fusion.7
  7.5 1.1 concatenate.9
  8.6 0.8 pad.10.y_ref
  9.4 1.5 %copy.15.x_ref = bf16[6144,32]{1,0:T(8,128)(2,1)} copy(bf16[6144,32]{0,1:T(8,128)(2,1)S(1)} %pad_bitcast_fusion) | data formatting | bytes 786432 | tf_op jit(solution)/shard_map/transpose | solution.py:40
  10.9 97.7 %shard_map.68 = (f32[3,16,256]{2,1,0:T(8,128)}, f32[3,16,256]{2,1,0:T(8,128)}, bf16[3,6,1024,1024]{3,2,1,0:T(8,128)(2,1)}) custom-call(bf16[6144,32]{1,0:T(8,128)(2,1)} %copy.15.x_ref, bf16[32,6144]{1,0:T(8,128)(2,1)} %pad.10.y_ref, bf16[3,16,256]{2,1,0:T(8,128)(2,1)} %copy_bitcast_fusion.6.u_ref, f32[3,16,256]{2,1,0:T(8,128)} %copy_bitcast_fusion.4.cm_ref, ...), custom_call_target="tpu_custom_call" | custom-call | tf_op jit(solution)/shard_map/pallas_call | solution.py:271
  108.6 0.8 copy_bitcast_fusion.2
  109.4 0.6 copy.21
  110.1 0.8 copy_bitcast_fusion.1
  110.9 0.6 copy.22
  (5 shorter events, 0.1 us)
Async XLA Ops:
  0.6 1.5 %copy-start = (f32[32,6144]{1,0:T(8,128)S(1)}, f32[32,6144]{1,0:T(8,128)}, u32[]{:S(2)}) copy-start(f32[32,6144]{1,0:T(8,128)} %param.9) | copy-start | bytes 2359300

commit v2 on v0

v2 whole, which is shorter than its diff:
```python
import functools
import math

import jax
import jax.numpy as jnp
from jax import lax
from jax.experimental import pallas as pl
from jax.experimental.pallas import tpu as pltpu
from jax.sharding import PartitionSpec as P

F32, BF16 = jnp.float32, jnp.bfloat16
MESH = pl.DeviceIdType.MESH
RATE = 100.0 / math.log(2.0)
TILE = 1024
CHUNKS = 3
DEPTH = 128
LANES = 128


def split3(values):
    first = values.astype(BF16).astype(F32)
    rest = values - first
    second = rest.astype(BF16).astype(F32)
    return first, second, rest - second


def kernel(
    total, xc_ref, yc_ref, sc_ref, rm_ref, cm_ref,
    new_ref, tgt_ref, far_ref,
    near, stage, x_fac, y_fac, u_in, v_in, u_all, v_all, shuffle, col_acc, row_acc, col_mass, row_mass,
    col_out, col_in, row_out, row_x, row_half, row_in,
    stage_sem, u_send, u_recv, v_send, v_recv, col_send, col_recv, x_send, x_recv, row_send, row_recv,
):
    src, tgt = lax.axis_index("src"), lax.axis_index("tgt")
    peers = lax.axis_size("src")
    weights = 2 * peers
    pts = sc_ref.shape[1]
    blocks = tiles = pts // TILE
    stored = near.shape[0]
    span = pts // CHUNKS
    half = peers // 2
    xh, z = lax.div(tgt, half), lax.rem(tgt, half)

    def each_peer(body, count=peers):
        def step(r, carry):
            body(r)
            return carry
        lax.fori_loop(1, count, step, 0)

    barrier = pltpu.get_barrier_semaphore()

    def greet(r):
        pl.semaphore_signal(barrier, inc=1, device_id={"src": lax.rem(src + r, peers)}, device_id_type=MESH)
        pl.semaphore_signal(barrier, inc=1, device_id={"tgt": lax.rem(tgt + r, peers)}, device_id_type=MESH)

    each_peer(greet)

    def folded(out, rows_of, at, cols):
        wide = cols // LANES
        for w in range(2):
            for k in range(wide):
                out[w * wide + k:w * wide + k + 1, :] = rows_of(w, at + k * LANES)

    def unfolded(ref, at, value):
        wide = value.shape[0] // 2
        for w in range(2):
            for k in range(wide):
                ref[w:w + 1, pl.ds(at + k * LANES, LANES)] = value[w * wide + k:w * wide + k + 1, :]

    def ordered(parts, all_ref, at, cols):
        wide = cols // LANES
        for d in range(peers):
            shuffle[d * 2 * wide:(d + 1) * 2 * wide, :] = parts[d].astype(F32)
        for k in range(wide):
            lanes = at + k * LANES
            all_ref[:, lanes:lanes + LANES] = shuffle[pl.ds(k, weights, stride=wide), :].astype(BF16)

    def scattered(acc, at, cols, out):
        wide = cols // LANES
        for k in range(wide):
            out[pl.ds(k, weights, stride=wide), :] = acc[:, pl.ds(at + k * LANES, LANES)]

    folded(shuffle, lambda w, lane: sc_ref[w:w + 1, lane:lane + LANES], 0, pts)
    u_in[tgt] = shuffle[:u_in.shape[1], :].astype(BF16)
    group = cm_ref[pl.ds(pl.multiple_of(lax.div(src, 4) * 8, 8), 8), :]
    place = lax.rem(src, 4)
    own = jnp.where(place < 2, jnp.where(place == 0, group[0:2], group[2:4]), jnp.where(place == 2, group[4:6], group[6:8]))
    for c in range(CHUNKS):
        folded(col_mass.at[c], lambda w, lane: own[w:w + 1, lane:lane + LANES], c * span, span)
    for c in range(tiles):
        folded(row_mass.at[c], lambda w, lane: rm_ref[w:w + 1, lane:lane + LANES], c * TILE, TILE)

    pl.semaphore_wait(barrier, 2 * (peers - 1))

    def gather_copy(buf, axis, me, r, send, recv):
        return pltpu.make_async_remote_copy(
            src_ref=buf.at[me], dst_ref=buf.at[me], send_sem=send, recv_sem=recv,
            device_id={axis: lax.rem(me + r, peers)}, device_id_type=MESH,
        )

    def group_copy(group, axis, peer, send, recv):
        return pltpu.make_async_remote_copy(
            src_ref=group, dst_ref=group, send_sem=send, recv_sem=recv,
            device_id={axis: peer}, device_id_type=MESH,
        )

    def u_group():
        return group_copy(u_in.at[pl.ds(0, peers - 1)], "tgt", lax.rem(tgt + 1, peers), u_send, u_recv)

    def v_group(c):
        return group_copy(v_in.at[c, pl.ds(0, peers - 1)], "src", lax.rem(src + 1, peers), v_send.at[c], v_recv.at[c])

    def col_group(c):
        return group_copy(col_in.at[c], "src", lax.rem(src + 1, peers), col_send.at[c], col_recv.at[c])

    def row_group(c):
        return group_copy(row_in.at[c], "tgt", xh * half + lax.rem(z + 1, half), row_send.at[c], row_recv.at[c])

    each_peer(lambda r: gather_copy(u_in, "tgt", tgt, r, u_send, u_recv).start())

    def factor_rows(out, parts, own_at, ones_at, own):
        for n, part in enumerate(parts):
            out[3 * n:3 * n + 3, :] = part
        for n, part in enumerate(own):
            out[own_at + n:own_at + n + 1, :] = part
            out[ones_at + n:ones_at + n + 1, :] = jnp.ones_like(part)
        out[30:32, :] = jnp.zeros((2, pts), F32)

    def squares(values):
        return values[0:1] * values[0:1] + values[1:2] * values[1:2] + values[2:3] * values[2:3]

    xc, yc = xc_ref[...] - 0.5, yc_ref[...] - 0.5
    xs, ys = split3((2.0 * RATE) * xc), split3(yc)
    pairs = ((0, 0), (0, 1), (1, 0), (1, 1), (0, 2), (2, 0), (1, 2), (2, 1))
    factor_rows(col_acc, [xs[p] for p, _ in pairs], 24, 27, split3(-RATE * squares(xc)))
    factor_rows(row_acc, [ys[q] for _, q in pairs], 27, 24, split3(math.log2(180.0) - RATE * squares(yc)))

    def rows_at(i):
        return pl.ds(pl.multiple_of(i * TILE, TILE), TILE)

    def lay(i, carry):
        zeros = jnp.zeros((DEPTH - 32, TILE), F32)
        x_fac[rows_at(i), :] = jnp.concatenate([col_acc[0:32, rows_at(i)], zeros], 0).T.astype(BF16)
        y_fac[0:32, rows_at(i)] = row_acc[0:32, rows_at(i)].astype(BF16)
        y_fac[32:, rows_at(i)] = zeros.astype(BF16)
        return carry

    lax.fori_loop(0, tiles, lay, 0)

    def make_tile(b, i):
        e = jnp.dot(x_fac[rows_at(i), :], y_fac[:, rows_at(b)], preferred_element_type=F32)
        return jnp.exp2(e).astype(BF16)

    def make_only(t, carry):
        b, i = lax.div(t, tiles), lax.rem(t, tiles)
        near[b, rows_at(i), :] = make_tile(b, i)
        return carry

    def use_only(b):
        def step(i, acc):
            return acc + jnp.dot(u_all[:, rows_at(i)], near[b, rows_at(i), :], preferred_element_type=F32)
        col_acc[:, b * TILE:(b + 1) * TILE] = lax.fori_loop(0, tiles, step, jnp.zeros((weights, TILE), F32))

    def stored_copy(slot, f, i):
        return pltpu.make_async_copy(stage.at[slot], far_ref.at[f, i], stage_sem.at[slot])

    def make_and_use(b):
        f = b - stored

        def step(i, acc):
            slot = lax.rem(i, 3)
            tile = make_tile(b, i)
            if f == 0:
                @pl.when(i >= 3)
                def _():
                    stored_copy(slot, f, 0).wait()
            else:
                stored_copy(slot, f, 0).wait()
            stage[slot] = tile
            stored_copy(slot, f, i).start()
            return acc + jnp.dot(u_all[:, rows_at(i)], tile, preferred_element_type=F32)
        col_acc[:, b * TILE:(b + 1) * TILE] = lax.fori_loop(0, tiles, step, jnp.zeros((weights, TILE), F32))

    def send_cols(c):
        scattered(col_acc, c * span, span, col_out.at[c])
        rows = 2 * span // LANES

        def send(r):
            peer = lax.rem(src + r, peers)
            pltpu.make_async_remote_copy(
                src_ref=col_out.at[c, pl.ds(pl.multiple_of(peer * rows, rows), rows)], dst_ref=col_in.at[c, r - 1],
                send_sem=col_send.at[c], recv_sem=col_recv.at[c],
                device_id={"src": peer}, device_id_type=MESH,
            ).start()
        each_peer(send)

    def turn_cols(c):
        rows = 2 * span // LANES
        col_group(c).wait_recv()
        value = col_out[c, pl.ds(pl.multiple_of(src * rows, rows), rows)]
        for r in range(peers - 1):
            value = value + col_in[c, r]
        value = col_mass[c] / (value / total)
        v_in[c, src] = value.astype(BF16)
        each_peer(lambda r: gather_copy(v_in.at[c], "src", src, r, v_send.at[c], v_recv.at[c]).start())
        unfolded(tgt_ref, c * span, value)

    def take_cols(c):
        v_group(c).wait_recv()
        ordered(v_in.at[c], v_all, c * span, span)

    lax.fori_loop(0, stored * tiles, make_only, 0)
    u_group().wait_recv()
    ordered(u_in, u_all, 0, pts)
    use_only(0)
    use_only(1)
    send_cols(0)
    use_only(2)
    make_and_use(3)
    send_cols(1)
    turn_cols(0)
    make_and_use(4)
    turn_cols(1)
    make_and_use(5)
    send_cols(2)

    count = (blocks - stored) * tiles

    def fetch(t):
        early = t < tiles
        f = jnp.where(early, 0, 1 + lax.rem(t, 2))
        i = jnp.where(early, t, lax.div(t - tiles, 2))
        slot = lax.rem(t, 3)
        return pltpu.make_async_copy(far_ref.at[f, i], stage.at[slot], stage_sem.at[slot])

    def fetch_later(t):
        @pl.when(t < count)
        def _():
            fetch(t).start()

    for slot in range(3):
        stored_copy(slot, 0, 0).wait()
    for t in range(3):
        fetch(t).start()

    def by_rows(b, tile):
        return lax.dot_general(
            v_all[:, b * TILE:(b + 1) * TILE], tile, (((1,), (1,)), ((), ())), preferred_element_type=F32
        )

    def near_block(b):
        def step(i, carry):
            part = by_rows(b, near[b, rows_at(i), :])
            if b == 0:
                row_acc[:, rows_at(i)] = part
            else:
                row_acc[:, rows_at(i)] += part
            return carry
        lax.fori_loop(0, tiles, step, 0)

    def far_step(t, carry):
        fetch(t).wait()
        row_acc[:, rows_at(t)] += by_rows(stored, stage[lax.rem(t, 3)])
        fetch_later(t + 3)
        return carry

    own_rows = 2 * TILE // LANES
    half_rows = half * own_rows

    def cross(c):
        return pltpu.make_async_remote_copy(
            src_ref=row_out.at[c, pl.ds(pl.multiple_of((1 - xh) * half_rows, half_rows), half_rows)], dst_ref=row_x.at[c],
            send_sem=x_send.at[c], recv_sem=x_recv.at[c],
            device_id={"tgt": lax.rem(tgt + half, peers)}, device_id_type=MESH,
        )

    def along(c):
        cross(c).wait_recv()
        row_half[c] = row_out[c, pl.ds(pl.multiple_of(xh * half_rows, half_rows), half_rows)] + row_x[c]

        def send(r):
            to = lax.rem(z + r, half)
            pltpu.make_async_remote_copy(
                src_ref=row_half.at[c, pl.ds(pl.multiple_of(to * own_rows, own_rows), own_rows)], dst_ref=row_in.at[c, r - 1],
                send_sem=row_send.at[c], recv_sem=row_recv.at[c],
                device_id={"tgt": xh * half + to}, device_id_type=MESH,
            ).start()
        each_peer(send, half)

    def last_step(c, carry):
        part = row_acc[:, rows_at(c)] + by_rows(2, near[2, rows_at(c), :])
        for n in range(2):
            t = tiles + 2 * c + n
            fetch(t).wait()
            part = part + by_rows(stored + 1 + n, stage[lax.rem(t, 3)])
            fetch_later(t + 3)
        row_acc[:, rows_at(c)] = part
        scattered(row_acc, c * TILE, TILE, row_out.at[c])
        cross(c).start()

        @pl.when(c > 0)
        def _():
            along(c - 1)
        return carry

    take_cols(0)
    near_block(0)
    near_block(1)
    turn_cols(2)
    take_cols(1)
    lax.fori_loop(0, tiles, far_step, 0)
    take_cols(2)
    lax.fori_loop(0, tiles, last_step, 0)
    along(tiles - 1)

    def finish(c, carry):
        row_group(c).wait_recv()
        value = row_half[c, pl.ds(pl.multiple_of(z * own_rows, own_rows), own_rows)]
        for r in range(half - 1):
            value = value + row_in[c, r]
        unfolded(new_ref, pl.multiple_of(c * TILE, TILE), row_mass[c] / (value / total))
        row_group(c).wait_send()
        cross(c).wait_send()
        return carry

    lax.fori_loop(0, tiles, finish, 0)
    u_group().wait_send()
    for c in range(CHUNKS):
        col_group(c).wait_send()
        v_group(c).wait_send()


def on_device(src_coords, tgt_coords, src_scaling, src_mass, tgt_mass):
    pts = src_coords.shape[1]
    weights = tgt_mass.shape[0]
    peers = lax.axis_size("src")
    total = float(pts * peers)
    tiles = pts // TILE
    stored = tiles // 2
    span = pts // CHUNKS
    half = peers // 2
    piece, tile_piece = 2 * span // LANES, 2 * TILE // LANES
    vmem = pl.BlockSpec(memory_space=pltpu.VMEM)
    dma = pltpu.SemaphoreType.DMA
    scratch = [
        ((stored, pts, TILE), BF16),
        ((3, TILE, TILE), BF16),
        ((pts, DEPTH), BF16),
        ((DEPTH, pts), BF16),
        ((peers, 2 * pts // LANES, LANES), BF16),
        ((CHUNKS, peers, piece, LANES), BF16),
        ((weights, pts), BF16),
        ((weights, pts), BF16),
        ((weights * pts // LANES, LANES), F32),
        ((weights, pts), F32),
        ((weights, pts), F32),
        ((CHUNKS, piece, LANES), F32),
        ((tiles, tile_piece, LANES), F32),
        ((CHUNKS, peers * piece, LANES), F32),
        ((CHUNKS, peers - 1, piece, LANES), F32),
        ((tiles, peers * tile_piece, LANES), F32),
        ((tiles, half * tile_piece, LANES), F32),
        ((tiles, half * tile_piece, LANES), F32),
        ((tiles, half - 1, tile_piece, LANES), F32),
    ]
    new, out, _ = pl.pallas_call(
        functools.partial(kernel, total),
        out_shape=(
            jax.ShapeDtypeStruct((2, pts), F32),
            jax.ShapeDtypeStruct((2, pts), F32),
            jax.ShapeDtypeStruct((tiles - stored, tiles, TILE, TILE), BF16),
        ),
        in_specs=[vmem] * 5,
        out_specs=(vmem, vmem, pl.BlockSpec(memory_space=pl.ANY)),
        scratch_shapes=[pltpu.VMEM(shape, dtype) for shape, dtype in scratch] + [
            dma((3,)), dma, dma, dma((CHUNKS,)), dma((CHUNKS,)), dma((CHUNKS,)), dma((CHUNKS,)),
            dma((tiles,)), dma((tiles,)), dma((tiles,)), dma((tiles,)),
        ],
        compiler_params=pltpu.CompilerParams(
            collective_id=0, has_side_effects=True, vmem_limit_bytes=60 * 2**20
        ),
    )(src_coords, tgt_coords, src_scaling, src_mass, tgt_mass)
    return new, out


def solution(mesh):
    placed = (P(None, "src"), P(None, "tgt"), P("tgt", "src"), P("tgt", "src"), P(None, "tgt"))
    return jax.shard_map(
        on_device,
        mesh=mesh,
        in_specs=placed,
        out_specs=(P("tgt", "src"), P("src", "tgt")),
        check_vma=False,
    )
```

time: 513 us -> 102 us (0.20)
  waiting for transfers between devices: 270 us -> 0 us
  matrix products: 130 us -> 0 us
  Pallas kernels: 0 us -> 98.2 us
  blocking collectives: 65.7 us -> 0 us
  local copies, waits for them, and re-layouts: 25.7 us -> 2.84 us
  between operations: 15.4 us -> 0.64 us
    unnamed x4 -> x0, waiting for transfers between devices: 270 us -> none
    dot_general x24 -> x0, matrix products: 130 us -> none  [the longest x12 66.3 us: col_step(): return (carry + jnp.dot(ub, kern, preferred_element_type=jnp.float32), None)]
    pallas_call x0 -> x1, Pallas kernels: none -> 98.2 us  [on_device(): pl.pallas_call(functools.partial(kernel, total), out_shape=(jax.ShapeDtyp...]
    all_gather x2 -> x0, blocking collectives: 65.7 us -> none  [the longest x1 46.1 us: on_device(): lax.all_gather(src_scaling.astype(jnp.bfloat16), 'tgt', axis=0, tiled=True)]
    slice x48 -> x0, local copies, waits for them, and re-layouts: 21 us -> none  [kernel_block(): dist = (xb[0][:, None] - yt[0][None, :]) ** 2]
  transfers between devices with their start and end apart: 2 -> 0, of which waited for: 2 -> 0; matrix products, arithmetic and copies ran while one was open for 0% -> 0% of each run, Pallas kernels for 0% -> 0%
where the time goes in v2:
time: 102 us
  Pallas kernels  98.2 us (96%)
  local copies, waits for them, and re-layouts  2.84 us (3%)
    pallas_call x1, Pallas kernels, on_device(): pl.pallas_call(functools.partial(kernel, total), out_shape=(jax.ShapeDtyp...  98.2 us
    unnamed x2, local copies, waits for them, and re-layouts  2.84 us

profile of v2, /device:TPU:16, one launch (start us, length us, event | category | flops | bytes accessed | tf_op | source)
XLA Modules:
  0.0 101.7 jit_solution(11848218022313714638)
XLA Ops:
  0.6 98.2 %shard_map.68 = (f32[2,6144]{1,0:T(2,128)}, f32[2,6144]{1,0:T(2,128)}, bf16[3,6,1024,1024]{3,2,1,0:T(8,128)(2,1)}) custom-call(f32[3,6144]{1,0:T(4,128)} %xc_ref.1, f32[3,6144]{1,0:T(4,128)} %yc_ref.1, f32[2,6144]{1,0:T(2,128)} %sc_ref.1, f32[2,6144]{1,0:T(2,128)} %rm_ref.1, f32[32,6144]{1,0:T(8,128)} %cm_ref.1), custom_call_target="tpu_custom_call" | custom-call | tf_op jit(solution)/shard_map/pallas_call | solution.py:366
  98.9 1.4 %copy.9 = f32[2,6144]{1,0:T(2,128)} copy(f32[2,6144]{1,0:T(2,128)} %get-tuple-element.8) | data formatting | bytes 98304
  100.3 1.4 %copy.10 = f32[2,6144]{1,0:T(2,128)} copy(f32[2,6144]{1,0:T(2,128)} %get-tuple-element.9) | data formatting | bytes 98304

commit v3 on v2

--- a/solution.py
+++ b/solution.py
@@ -12,6 +12,7 @@
 MESH = pl.DeviceIdType.MESH
 RATE = 100.0 / math.log(2.0)
 TILE = 1024
+PIECE = 256
 CHUNKS = 3
 DEPTH = 128
 LANES = 128
@@ -27,7 +28,7 @@
 def kernel(
     total, xc_ref, yc_ref, sc_ref, rm_ref, cm_ref,
     new_ref, tgt_ref, far_ref,
-    near, stage, x_fac, y_fac, u_in, v_in, u_all, v_all, shuffle, col_acc, row_acc, col_mass, row_mass,
+    near0, near1, near2, stage0, stage1, stage2, x_fac, y_fac, u_in, v_in, u_all, v_all, shuffle, col_acc, row_acc, col_mass, row_mass,
     col_out, col_in, row_out, row_x, row_half, row_in,
     stage_sem, u_send, u_recv, v_send, v_recv, col_send, col_recv, x_send, x_recv, row_send, row_recv,
 ):
@@ -36,7 +37,8 @@
     weights = 2 * peers
     pts = sc_ref.shape[1]
     blocks = tiles = pts // TILE
-    stored = near.shape[0]
+    near, stage = (near0, near1, near2), (stage0, stage1, stage2)
+    slots, far = len(stage), blocks - len(near)
     span = pts // CHUNKS
     half = peers // 2
     xh, z = lax.div(tgt, half), lax.rem(tgt, half)
@@ -147,39 +149,58 @@
 
     lax.fori_loop(0, tiles, lay, 0)
 
-    def make_tile(b, i):
-        e = jnp.dot(x_fac[rows_at(i), :], y_fac[:, rows_at(b)], preferred_element_type=F32)
+    def make_piece(start, b, i):
+        rows = pl.ds(pl.multiple_of(i * TILE + start, PIECE), PIECE)
+        e = jnp.dot(x_fac[rows, :], y_fac[:, rows_at(b)], preferred_element_type=F32)
         return jnp.exp2(e).astype(BF16)
 
-    def make_only(t, carry):
-        b, i = lax.div(t, tiles), lax.rem(t, tiles)
-        near[b, rows_at(i), :] = make_tile(b, i)
-        return carry
+    def make_only(b):
+        def step(i, carry):
+            e = jnp.dot(x_fac[rows_at(i), :], y_fac[:, b * TILE:(b + 1) * TILE], preferred_element_type=F32)
+            near[b - far][rows_at(i), :] = jnp.exp2(e).astype(BF16)
+            return carry
+        lax.fori_loop(0, tiles, step, 0)
 
     def use_only(b):
         def step(i, acc):
-            return acc + jnp.dot(u_all[:, rows_at(i)], near[b, rows_at(i), :], preferred_element_type=F32)
+            return acc + jnp.dot(u_all[:, rows_at(i)], near[b - far][rows_at(i), :], preferred_element_type=F32)
         col_acc[:, b * TILE:(b + 1) * TILE] = lax.fori_loop(0, tiles, step, jnp.zeros((weights, TILE), F32))
 
-    def stored_copy(slot, f, i):
-        return pltpu.make_async_copy(stage.at[slot], far_ref.at[f, i], stage_sem.at[slot])
-
-    def make_and_use(b):
-        f = b - stored
-
+    def make_and_use(made, used):
         def step(i, acc):
-            slot = lax.rem(i, 3)
-            tile = make_tile(b, i)
-            if f == 0:
-                @pl.when(i >= 3)
+            for start in range(0, TILE, PIECE):
+                rows = pl.ds(pl.multiple_of(i * TILE + start, PIECE), PIECE)
+                near[made - far][rows, :] = make_piece(start, made, i)
+                acc = acc + jnp.dot(u_all[:, rows], near[used - far][rows, :], preferred_element_type=F32)
+            return acc
+        col_acc[:, used * TILE:(used + 1) * TILE] = lax.fori_loop(0, tiles, step, jnp.zeros((weights, TILE), F32))
+
+    def stored_copy(slot, t):
+        return pltpu.make_async_copy(stage[slot], far_ref.at[lax.div(t, tiles), lax.rem(t, tiles)], stage_sem.at[slot])
+
+    def far_steps(first, last):
+        def step(n, carry):
+            for slot in range(slots):
+                t = n * slots + slot
+                b, i = lax.div(t, tiles), lax.rem(t, tiles)
+                other = (slot + 1) % slots
+                later = jnp.minimum(t + 1, far * tiles - 1)
+                lb, li = lax.div(later, tiles), lax.rem(later, tiles)
+
+                @pl.when(t + 1 >= slots)
                 def _():
-                    stored_copy(slot, f, 0).wait()
-            else:
-                stored_copy(slot, f, 0).wait()
-            stage[slot] = tile
-            stored_copy(slot, f, i).start()
-            return acc + jnp.dot(u_all[:, rows_at(i)], tile, preferred_element_type=F32)
-        col_acc[:, b * TILE:(b + 1) * TILE] = lax.fori_loop(0, tiles, step, jnp.zeros((weights, TILE), F32))
+                    stored_copy(other, 0).wait()
+
+                stored_copy(slot, t).start()
+                acc = jnp.zeros((weights, TILE), F32)
+                for start in range(0, TILE, PIECE):
+                    piece = slice(start, start + PIECE)
+                    stage[other][piece, :] = make_piece(start, lb, li)
+                    rows = pl.ds(pl.multiple_of(i * TILE + start, PIECE), PIECE)
+                    acc = acc + jnp.dot(u_all[:, rows], stage[slot][piece, :], preferred_element_type=F32)
+                col_acc[:, rows_at(b)] += acc
+            return carry
+        lax.fori_loop(first // slots, last // slots, step, 0)
 
     def send_cols(c):
         scattered(col_acc, c * span, span, col_out.at[c])
@@ -209,60 +230,63 @@
         v_group(c).wait_recv()
         ordered(v_in.at[c], v_all, c * span, span)
 
-    lax.fori_loop(0, stored * tiles, make_only, 0)
+    make_only(3)
+    make_only(4)
+    for start in range(0, TILE, PIECE):
+        stage[0][start:start + PIECE, :] = make_piece(start, 0, 0)
     u_group().wait_recv()
     ordered(u_in, u_all, 0, pts)
-    use_only(0)
-    use_only(1)
+    col_acc[:, :far * TILE] = jnp.zeros((weights, far * TILE), F32)
+    far_steps(0, 2 * tiles)
     send_cols(0)
-    use_only(2)
-    make_and_use(3)
+    far_steps(2 * tiles, 3 * tiles)
+    make_and_use(5, 3)
     send_cols(1)
     turn_cols(0)
-    make_and_use(4)
-    turn_cols(1)
-    make_and_use(5)
+    use_only(4)
+    use_only(5)
     send_cols(2)
 
-    count = (blocks - stored) * tiles
-
-    def fetch(t):
-        early = t < tiles
-        f = jnp.where(early, 0, 1 + lax.rem(t, 2))
-        i = jnp.where(early, t, lax.div(t - tiles, 2))
-        slot = lax.rem(t, 3)
-        return pltpu.make_async_copy(far_ref.at[f, i], stage.at[slot], stage_sem.at[slot])
-
-    def fetch_later(t):
+    count = far * tiles
+
+    def fetch(slot, t):
+        return pltpu.make_async_copy(far_ref.at[lax.div(t, tiles), lax.rem(t, tiles)], stage[slot], stage_sem.at[slot])
+
+    def fetch_later(slot, t):
         @pl.when(t < count)
         def _():
-            fetch(t).start()
-
-    for slot in range(3):
-        stored_copy(slot, 0, 0).wait()
-    for t in range(3):
-        fetch(t).start()
+            fetch(slot, t).start()
+
+    for slot in range(1, slots):
+        stored_copy(slot, 0).wait()
+    for t in range(slots):
+        fetch(t, t).start()
 
     def by_rows(b, tile):
         return lax.dot_general(
-            v_all[:, b * TILE:(b + 1) * TILE], tile, (((1,), (1,)), ((), ())), preferred_element_type=F32
+            v_all[:, b], tile, (((1,), (1,)), ((), ())), preferred_element_type=F32
         )
 
-    def near_block(b):
+    def far_rows(first, last, fresh):
+        def step(n, carry):
+            for slot in range(slots):
+                t = n * slots + slot
+                i = lax.rem(t, tiles)
+                fetch(slot, t).wait()
+                part = by_rows(rows_at(lax.div(t, tiles)), stage[slot][...])
+                if fresh:
+                    row_acc[:, rows_at(i)] = part
+                else:
+                    row_acc[:, rows_at(i)] += part
+                fetch_later(slot, t + slots)
+            return carry
+        lax.fori_loop(first // slots, last // slots, step, 0)
+
+    def near_rows(b):
         def step(i, carry):
-            part = by_rows(b, near[b, rows_at(i), :])
-            if b == 0:
-                row_acc[:, rows_at(i)] = part
-            else:
-                row_acc[:, rows_at(i)] += part
+            row_acc[:, rows_at(i)] += by_rows(slice(b * TILE, (b + 1) * TILE), near[b - far][rows_at(i), :])
             return carry
         lax.fori_loop(0, tiles, step, 0)
-
-    def far_step(t, carry):
-        fetch(t).wait()
-        row_acc[:, rows_at(t)] += by_rows(stored, stage[lax.rem(t, 3)])
-        fetch_later(t + 3)
-        return carry
 
     own_rows = 2 * TILE // LANES
     half_rows = half * own_rows
@@ -287,30 +311,35 @@
             ).start()
         each_peer(send, half)
 
-    def last_step(c, carry):
-        part = row_acc[:, rows_at(c)] + by_rows(2, near[2, rows_at(c), :])
-        for n in range(2):
-            t = tiles + 2 * c + n
-            fetch(t).wait()
-            part = part + by_rows(stored + 1 + n, stage[lax.rem(t, 3)])
-            fetch_later(t + 3)
-        row_acc[:, rows_at(c)] = part
-        scattered(row_acc, c * TILE, TILE, row_out.at[c])
-        cross(c).start()
-
-        @pl.when(c > 0)
-        def _():
-            along(c - 1)
+    def last_steps(n, carry):
+        for slot in range(slots):
+            c = n * slots + slot
+            part = row_acc[:, rows_at(c)]
+            for b in (4, 5):
+                part = part + by_rows(slice(b * TILE, (b + 1) * TILE), near[b - far][rows_at(c), :])
+            t = 2 * tiles + c
+            fetch(slot, t).wait()
+            part = part + by_rows(slice(2 * TILE, 3 * TILE), stage[slot][...])
+            fetch_later(slot, t + slots)
+            row_acc[:, rows_at(c)] = part
+            scattered(row_acc, pl.multiple_of(c * TILE, TILE), TILE, row_out.at[c])
+            cross(c).start()
+
+            @pl.when(c > 0)
+            def _():
+                along(c - 1)
         return carry
 
     take_cols(0)
-    near_block(0)
-    near_block(1)
+    far_rows(0, tiles, True)
+    turn_cols(1)
+    far_rows(tiles, tiles + slots, False)
     turn_cols(2)
+    far_rows(tiles + slots, 2 * tiles, False)
     take_cols(1)
-    lax.fori_loop(0, tiles, far_step, 0)
+    near_rows(3)
     take_cols(2)
-    lax.fori_loop(0, tiles, last_step, 0)
+    lax.fori_loop(0, tiles // slots, last_steps, 0)
     along(tiles - 1)
 
     def finish(c, carry):
@@ -343,8 +372,8 @@
     vmem = pl.BlockSpec(memory_space=pltpu.VMEM)
     dma = pltpu.SemaphoreType.DMA
     scratch = [
-        ((stored, pts, TILE), BF16),
-        ((3, TILE, TILE), BF16),
+        *[((pts, TILE), BF16)] * stored,
+        *[((TILE, TILE), BF16)] * 3,
         ((pts, DEPTH), BF16),
         ((DEPTH, pts), BF16),
         ((peers, 2 * pts // LANES, LANES), BF16),

time: 102 us -> 101 us (level)
  no operation moved by 1% of the time
where the time goes in v3:
time: 101 us
  Pallas kernels  97.6 us (97%)
  local copies, waits for them, and re-layouts  2.84 us (3%)
    pallas_call x1, Pallas kernels, on_device(): pl.pallas_call(functools.partial(kernel, total), out_shape=(jax.ShapeDtyp...  97.6 us
    unnamed x2, local copies, waits for them, and re-layouts  2.84 us

profile of v3, /device:TPU:16, one launch (start us, length us, event | category | flops | bytes accessed | tf_op | source)
XLA Modules:
  0.0 101.1 jit_solution(15348380986983116124)
XLA Ops:
  0.6 97.6 %shard_map.68 = (f32[2,6144]{1,0:T(2,128)}, f32[2,6144]{1,0:T(2,128)}, bf16[3,6,1024,1024]{3,2,1,0:T(8,128)(2,1)}) custom-call(f32[3,6144]{1,0:T(4,128)} %xc_ref.1, f32[3,6144]{1,0:T(4,128)} %yc_ref.1, f32[2,6144]{1,0:T(2,128)} %sc_ref.1, f32[2,6144]{1,0:T(2,128)} %rm_ref.1, f32[32,6144]{1,0:T(8,128)} %cm_ref.1), custom_call_target="tpu_custom_call" | custom-call | tf_op jit(solution)/shard_map/pallas_call | solution.py:395
  98.3 1.4 %copy.9 = f32[2,6144]{1,0:T(2,128)} copy(f32[2,6144]{1,0:T(2,128)} %get-tuple-element.8) | data formatting | bytes 98304
  99.7 1.4 %copy.10 = f32[2,6144]{1,0:T(2,128)} copy(f32[2,6144]{1,0:T(2,128)} %get-tuple-element.9) | data formatting | bytes 98304

commit v4 on v3

--- a/solution.py
+++ b/solution.py
@@ -27,16 +27,17 @@
 
 def kernel(
     total, xc_ref, yc_ref, sc_ref, rm_ref, cm_ref,
-    new_ref, tgt_ref, far_ref,
+    out_ref, far_ref,
     near0, near1, near2, stage0, stage1, stage2, x_fac, y_fac, u_in, v_in, u_all, v_all, shuffle, col_acc, row_acc, col_mass, row_mass,
-    col_out, col_in, row_out, row_x, row_half, row_in,
-    stage_sem, u_send, u_recv, v_send, v_recv, col_send, col_recv, x_send, x_recv, row_send, row_recv,
+    col_out, col_in, row_out, row_x, row_half, row_in, last_in,
+    stage_sem, u_send, u_recv, v_send, v_recv, col_send, col_recv, x_send, x_recv, row_send, row_recv, last_send, last_recv,
 ):
     src, tgt = lax.axis_index("src"), lax.axis_index("tgt")
     peers = lax.axis_size("src")
     weights = 2 * peers
     pts = sc_ref.shape[1]
     blocks = tiles = pts // TILE
+    new_ref, tgt_ref = out_ref.at[0], out_ref.at[1]
     near, stage = (near0, near1, near2), (stage0, stage1, stage2)
     slots, far = len(stage), blocks - len(near)
     span = pts // CHUNKS
@@ -311,6 +312,16 @@
             ).start()
         each_peer(send, half)
 
+    def last_send_all():
+        def send(r):
+            peer = lax.rem(tgt + r, peers)
+            pltpu.make_async_remote_copy(
+                src_ref=row_out.at[tiles - 1, pl.ds(pl.multiple_of(peer * own_rows, own_rows), own_rows)],
+                dst_ref=last_in.at[r - 1], send_sem=last_send, recv_sem=last_recv,
+                device_id={"tgt": peer}, device_id_type=MESH,
+            ).start()
+        each_peer(send)
+
     def last_steps(n, carry):
         for slot in range(slots):
             c = n * slots + slot
@@ -323,7 +334,14 @@
             fetch_later(slot, t + slots)
             row_acc[:, rows_at(c)] = part
             scattered(row_acc, pl.multiple_of(c * TILE, TILE), TILE, row_out.at[c])
-            cross(c).start()
+
+            @pl.when(c < tiles - 1)
+            def _():
+                cross(c).start()
+
+            @pl.when(c == tiles - 1)
+            def _():
+                last_send_all()
 
             @pl.when(c > 0)
             def _():
@@ -340,7 +358,6 @@
     near_rows(3)
     take_cols(2)
     lax.fori_loop(0, tiles // slots, last_steps, 0)
-    along(tiles - 1)
 
     def finish(c, carry):
         row_group(c).wait_recv()
@@ -352,7 +369,14 @@
         cross(c).wait_send()
         return carry
 
-    lax.fori_loop(0, tiles, finish, 0)
+    lax.fori_loop(0, tiles - 1, finish, 0)
+    last = group_copy(last_in, "tgt", lax.rem(tgt + 1, peers), last_send, last_recv)
+    last.wait_recv()
+    value = row_out[tiles - 1, pl.ds(pl.multiple_of(tgt * own_rows, own_rows), own_rows)]
+    for r in range(peers - 1):
+        value = value + last_in[r]
+    unfolded(new_ref, (tiles - 1) * TILE, row_mass[tiles - 1] / (value / total))
+    last.wait_send()
     u_group().wait_send()
     for c in range(CHUNKS):
         col_group(c).wait_send()
@@ -391,25 +415,25 @@
         ((tiles, half * tile_piece, LANES), F32),
         ((tiles, half * tile_piece, LANES), F32),
         ((tiles, half - 1, tile_piece, LANES), F32),
+        ((peers - 1, tile_piece, LANES), F32),
     ]
-    new, out, _ = pl.pallas_call(
+    out, _ = pl.pallas_call(
         functools.partial(kernel, total),
         out_shape=(
-            jax.ShapeDtypeStruct((2, pts), F32),
-            jax.ShapeDtypeStruct((2, pts), F32),
+            jax.ShapeDtypeStruct((2, 2, pts), F32),
             jax.ShapeDtypeStruct((tiles - stored, tiles, TILE, TILE), BF16),
         ),
         in_specs=[vmem] * 5,
-        out_specs=(vmem, vmem, pl.BlockSpec(memory_space=pl.ANY)),
+        out_specs=(vmem, pl.BlockSpec(memory_space=pl.ANY)),
         scratch_shapes=[pltpu.VMEM(shape, dtype) for shape, dtype in scratch] + [
             dma((3,)), dma, dma, dma((CHUNKS,)), dma((CHUNKS,)), dma((CHUNKS,)), dma((CHUNKS,)),
-            dma((tiles,)), dma((tiles,)), dma((tiles,)), dma((tiles,)),
+            dma((tiles,)), dma((tiles,)), dma((tiles,)), dma((tiles,)), dma, dma,
         ],
         compiler_params=pltpu.CompilerParams(
             collective_id=0, has_side_effects=True, vmem_limit_bytes=60 * 2**20
         ),
     )(src_coords, tgt_coords, src_scaling, src_mass, tgt_mass)
-    return new, out
+    return out[0], out[1]
 
 
 def solution(mesh):

time: 101 us -> 98.1 us (0.971)
  Pallas kernels: 97.6 us -> 95.8 us
  local copies, waits for them, and re-layouts: 2.84 us -> 1.47 us
    unnamed x2 -> x0, local copies, waits for them, and re-layouts: 2.84 us -> none
    pallas_call x1, Pallas kernels: 97.6 us -> 95.8 us  [on_device(): pl.pallas_call(functools.partial(kernel, total), out_shape=(jax.ShapeDtyp...]
    squeeze x0 -> x1, local copies, waits for them, and re-layouts: none -> 1.47 us  [on_device(): return (out[0], out[1])]
where the time goes in v4:
time: 98.1 us; the launch traced here: 97.9 us
  Pallas kernels  95.8 us (98%)
  local copies, waits for them, and re-layouts  1.47 us (1%)
    pallas_call x1, Pallas kernels, on_device(): pl.pallas_call(functools.partial(kernel, total), out_shape=(jax.ShapeDtyp...  95.8 us

profile of v4, /device:TPU:16, one launch (start us, length us, event | category | flops | bytes accessed | tf_op | source)
XLA Modules:
  0.0 97.9 jit_solution(15585751527914790466)
XLA Ops:
  0.6 95.8 %shard_map.68 = (f32[2,2,6144]{2,1,0:T(2,128)}, bf16[3,6,1024,1024]{3,2,1,0:T(8,128)(2,1)}) custom-call(f32[3,6144]{1,0:T(4,128)} %xc_ref.1, f32[3,6144]{1,0:T(4,128)} %yc_ref.1, f32[2,6144]{1,0:T(2,128)} %sc_ref.1, f32[2,6144]{1,0:T(2,128)} %rm_ref.1, f32[32,6144]{1,0:T(8,128)} %cm_ref.1), custom_call_target="tpu_custom_call" | custom-call | tf_op jit(solution)/shard_map/pallas_call | solution.py:420
  96.5 1.5 %slice_bitcast_fusion = (f32[2,6144]{1,0:T(2,128)}, f32[2,6144]{1,0:T(2,128)}) fusion(f32[2,2,6144]{2,1,0:T(2,128)} %get-tuple-element.3), kind=kLoop, calls=%fused_computation | loop fusion | bytes 196608 | tf_op jit(solution)/shard_map/squeeze | solution.py:436

commit v5 on v4

--- a/solution.py
+++ b/solution.py
@@ -165,7 +165,7 @@
     def use_only(b):
         def step(i, acc):
             return acc + jnp.dot(u_all[:, rows_at(i)], near[b - far][rows_at(i), :], preferred_element_type=F32)
-        col_acc[:, b * TILE:(b + 1) * TILE] = lax.fori_loop(0, tiles, step, jnp.zeros((weights, TILE), F32))
+        col_acc[:, b * TILE:(b + 1) * TILE] = lax.fori_loop(0, tiles, step, jnp.zeros((weights, TILE), F32), unroll=3)
 
     def make_and_use(made, used):
         def step(i, acc):
@@ -268,13 +268,13 @@
             v_all[:, b], tile, (((1,), (1,)), ((), ())), preferred_element_type=F32
         )
 
-    def far_rows(first, last, fresh):
+    def far_rows(b, first, last, fresh):
         def step(n, carry):
             for slot in range(slots):
                 t = n * slots + slot
                 i = lax.rem(t, tiles)
                 fetch(slot, t).wait()
-                part = by_rows(rows_at(lax.div(t, tiles)), stage[slot][...])
+                part = by_rows(slice(b * TILE, (b + 1) * TILE), stage[slot][...])
                 if fresh:
                     row_acc[:, rows_at(i)] = part
                 else:
@@ -287,7 +287,7 @@
         def step(i, carry):
             row_acc[:, rows_at(i)] += by_rows(slice(b * TILE, (b + 1) * TILE), near[b - far][rows_at(i), :])
             return carry
-        lax.fori_loop(0, tiles, step, 0)
+        lax.fori_loop(0, tiles, step, 0, unroll=3)
 
     own_rows = 2 * TILE // LANES
     half_rows = half * own_rows
@@ -349,11 +349,11 @@
         return carry
 
     take_cols(0)
-    far_rows(0, tiles, True)
+    far_rows(0, 0, tiles, True)
     turn_cols(1)
-    far_rows(tiles, tiles + slots, False)
+    far_rows(1, tiles, tiles + slots, False)
     turn_cols(2)
-    far_rows(tiles + slots, 2 * tiles, False)
+    far_rows(1, tiles + slots, 2 * tiles, False)
     take_cols(1)
     near_rows(3)
     take_cols(2)

time: 98.1 us -> 96.8 us (0.987)
  Pallas kernels: 95.8 us -> 94.4 us
    pallas_call x1, Pallas kernels: 95.8 us -> 94.4 us  [on_device(): pl.pallas_call(functools.partial(kernel, total), out_shape=(jax.ShapeDtyp...]
where the time goes in v5:
time: 96.8 us; the launch traced here: 96.5 us
  Pallas kernels  94.4 us (98%)
  local copies, waits for them, and re-layouts  1.47 us (2%)
    pallas_call x1, Pallas kernels, on_device(): pl.pallas_call(functools.partial(kernel, total), out_shape=(jax.ShapeDtyp...  94.4 us

profile of v5, /device:TPU:16, one launch (start us, length us, event | category | flops | bytes accessed | tf_op | source)
XLA Modules:
  0.0 96.5 jit_solution(8696394641576150581)
XLA Ops:
  0.6 94.4 %shard_map.68 = (f32[2,2,6144]{2,1,0:T(2,128)}, bf16[3,6,1024,1024]{3,2,1,0:T(8,128)(2,1)}) custom-call(f32[3,6144]{1,0:T(4,128)} %xc_ref.1, f32[3,6144]{1,0:T(4,128)} %yc_ref.1, f32[2,6144]{1,0:T(2,128)} %sc_ref.1, f32[2,6144]{1,0:T(2,128)} %rm_ref.1, f32[32,6144]{1,0:T(8,128)} %cm_ref.1), custom_call_target="tpu_custom_call" | custom-call | tf_op jit(solution)/shard_map/pallas_call | solution.py:420
  95.0 1.5 %slice_bitcast_fusion = (f32[2,6144]{1,0:T(2,128)}, f32[2,6144]{1,0:T(2,128)}) fusion(f32[2,2,6144]{2,1,0:T(2,128)} %get-tuple-element.3), kind=kLoop, calls=%fused_computation | loop fusion | bytes 196608 | tf_op jit(solution)/shard_map/squeeze | solution.py:436
